TPU v7x, 32 devices: a whole 2x2x4 slice. The times are simulated.
32 devices in a mesh: ta: 4 (over x, core), sa: 8 (over z, y).
Axes of the slice: x: 2, y: 2, z: 4, core: 2. Of those that a mesh axis runs over, the one named last changes fastest.
Arguments:
- video: bfloat16 [32, 8, 128, 1024], P('ta', 'sa'), may hold values from -6 to 6
- mix_gain: float32 [1024], replicated, may hold values from 0.1 to 1.9
- t_rate: float32 [1024], replicated, may hold values from 0.02 to 2
- s_kernel: float32 [15, 1024], replicated, may hold values from -2 to 2
- w_gate: bfloat16 [1024, 1024], replicated, may hold values from -0.1875 to 0.1875
- w_up: bfloat16 [1024, 1024], replicated, may hold values from -0.1875 to 0.1875
- w_down: bfloat16 [1024, 1024], replicated, may hold values from -0.1875 to 0.1875
Outputs:
- result: bfloat16 [32, 8, 128, 1024], P('ta', 'sa')
All inputs are finite; a program needn't handle non-finite values.
Results may differ from a plain program's by a relative error of at most 0.0063.
Values may be sent and summed in bfloat16 or wider, within the bound.
A program may use at most 128 MiB of HBM per device.

v0:
```python
import jax
import jax.numpy as jnp
from jax import lax
from jax.sharding import PartitionSpec as P

FB = 8


epsilon = 1e-06


def padded_2(block, sides, width):
    for axis, dim in sides:
        count = lax.axis_size(axis)
        forward = [(i, i + 1) for i in range(count - 1)]
        backward = [(target, source) for source, target in forward]
        low = lax.ppermute(
            lax.slice_in_dim(block, block.shape[dim] - width, None, axis=dim), axis, forward
        )
        high = lax.ppermute(lax.slice_in_dim(block, 0, width, axis=dim), axis, backward)
        block = jnp.concatenate([low, block, high], axis=dim)
    return block


def temporal(padded, decay_part):
    offsets = jnp.arange(-FB, FB + 1)
    kernel_taps = jnp.exp(-decay_part[None, :] * jnp.abs(offsets).astype(jnp.float32)[:, None])
    accum_sum = jnp.zeros((FB,) + padded.shape[1:], jnp.float32)
    for tap_index in range(2 * FB + 1):
        shift_by = tap_index - FB
        accum_sum = accum_sum + kernel_taps[tap_index] * padded[
            FB - shift_by : 2 * FB - shift_by
        ].astype(jnp.float32)
    return accum_sum


def spatial(local_block, s_kernel, channel_start, channel_share):
    height = local_block.shape[1]
    kernel_part = lax.dynamic_slice_in_dim(s_kernel, channel_start, channel_share, 1)
    row_ids = jnp.arange(height)
    offset_idx = row_ids[:, None] - row_ids[None, :] + height - 1
    toeplitz = jnp.take(kernel_part, offset_idx, axis=0)
    return jnp.einsum(
        "hkc,fkwc->fhwc", toeplitz, local_block.astype(jnp.float32), precision=lax.Precision.HIGHEST
    )


def body(video, mix_gain, t_rate, s_kernel, w_gate, w_up, w_down):
    channels = video.shape[3]
    widened_in = video.astype(jnp.float32)
    normed = (
        widened_in * lax.rsqrt(jnp.mean(widened_in * widened_in, -1, keepdims=True) + epsilon)
    ).astype(jnp.bfloat16)
    channel_share = channels // lax.axis_size("sa")
    channel_start = lax.axis_index("sa") * channel_share
    padded = padded_2(normed, (("ta", 0),), FB)
    temporal_mix = temporal(padded, t_rate)
    spatial_mix = spatial(
        lax.all_to_all(normed, "sa", split_axis=3, concat_axis=1, tiled=True),
        s_kernel,
        channel_start,
        channel_share,
    )
    spatial_mix = lax.all_to_all(spatial_mix, "sa", split_axis=1, concat_axis=3, tiled=True)
    summed = (temporal_mix + spatial_mix).astype(jnp.bfloat16)
    widened = lax.optimization_barrier(summed).astype(jnp.float32)
    normal_mix = (
        widened * lax.rsqrt(jnp.mean(widened * widened, -1, keepdims=True) + epsilon) * mix_gain
    ).astype(jnp.bfloat16)
    flat_rows = normal_mix.reshape(-1, channels)
    gate_act = jnp.dot(flat_rows, w_gate, preferred_element_type=jnp.float32)
    up_act = jnp.dot(flat_rows, w_up, preferred_element_type=jnp.float32)
    hidden = (jax.nn.silu(gate_act) * up_act).astype(jnp.bfloat16)
    output = widened_in.reshape(-1, channels) + jnp.dot(
        hidden, w_down, preferred_element_type=jnp.float32
    )
    return output.astype(jnp.bfloat16).reshape(video.shape)


def solution(mesh):
    in_specs = (P("ta", "sa", None, None), P(), P(), P(), P(), P(), P())
    out_specs = P("ta", "sa", None, None)
    return jax.shard_map(body, mesh=mesh, in_specs=in_specs, out_specs=out_specs, check_vma=False)
```

profile of v0, /device:TPU:0, one launch (start us, length us, event | category | flops | bytes accessed | tf_op | source)
XLA Modules:
  0.0 213.2 jit_solution(15158020561497334832)
XLA Ops:
  0.0 4.1 %copy.23 = bf16[8,1,128,1024]{2,3,0,1:T(8,128)(2,1)} copy(bf16[8,1,128,1024]{3,2,1,0:T(8,128)(2,1)} %param.7) | data formatting | bytes 4194304 | tf_op args[0]
  4.1 2.0 multiply_reduce_fusion
  6.1 2.0 multiply_convert_fusion.1
  8.1 0.0 copy-start.1
  8.1 1.3 copy-done.1
  9.4 2.7 %copy.25 = bf16[8,1,128,1024]{2,0,1,3:T(8,128)(2,1)} copy(bf16[8,1,128,1024]{2,3,0,1:T(8,128)(2,1)S(1)} %multiply_convert_fusion.1) | data formatting | bytes 4194304 | tf_op jit(solution)/shard_map/convert_element_type | solution.py:53
  12.1 7.3 %all-to-all-start = ((bf16[8,1,128,1024]{2,0,1,3:T(8,128)(2,1)}), bf16[8,1,128,1024]{2,0,1,3:T(8,128)(2,1)}, u32[]{:S(2)}, u32[]{:S(2)}) async-start(bf16[8,1,128,1024]{2,0,1,3:T(8,128)(2,1)} %copy.25), calls=%async_computation | async-start | bytes 4194304 | tf_op jit(solution)/shard_map/all_to_all | solution.py:59
  19.4 0.1 reshape.144
  19.5 0.7 constant_dynamic-slice_fusion
  20.2 0.6 gather_fusion
  20.8 0.2 copy.28
  21.0 46.7 %all-to-all-done = bf16[8,1,128,1024]{2,0,1,3:T(8,128)(2,1)} async-done(((bf16[8,1,128,1024]{2,0,1,3:T(8,128)(2,1)}), bf16[8,1,128,1024]{2,0,1,3:T(8,128)(2,1)}, u32[]{:S(2)}, u32[]{:S(2)}) %all-to-all-start) | async-done | bytes 2097184 | tf_op jit(solution)/shard_map/all_to_all | solution.py:59
  67.7 4.2 %convolution_bitcast_fusion = f32[8,8,128,128]{2,1,0,3:T(8,128)S(1)} fusion(bf16[8,1,128,8,128]{2,0,4,3,1:T(8,128)(2,1)} %bitcast.18, f32[8,8,128]{1,0,2:T(8,128)S(1)} %copy.28, pred[8,8]{1,0:T(8,128)(4,1)S(1)} %fusion.25), kind=kOutput, calls=%fused_computation.37 | convolution fusion | flops 100671488 | bytes 6324288 | tf_op jit(solution)/shard_map/hkc,fkwc->fhwc/dot_general | solution.py:43
  71.9 2.7 %copy.29 = f32[8,8,128,128]{2,0,3,1:T(8,128)} copy(f32[8,8,128,128]{2,1,0,3:T(8,128)S(1)} %convolution_bitcast_fusion) | data formatting | bytes 8388608 | tf_op jit(solution)/shard_map/hkc,fkwc->fhwc/transpose | solution.py:43
  74.7 4.6 %all-to-all-start.1 = ((f32[8,8,128,128]{2,0,3,1:T(8,128)}), f32[8,8,128,128]{2,0,3,1:T(8,128)}, u32[]{:S(2)}, u32[]{:S(2)}) async-start(f32[8,8,128,128]{2,0,3,1:T(8,128)} %copy.29), calls=%async_computation.1 | async-start | bytes 8388608 | tf_op jit(solution)/shard_map/all_to_all | solution.py:64
  79.2 0.0 copy-start.3
  79.2 1.3 collective-permute-start
  80.5 4.4 %collective-permute-start.1 = (bf16[8,1,128,1024]{2,3,0,1:T(8,128)(2,1)}, bf16[8,1,128,1024]{2,3,0,1:T(8,128)(2,1)}, u32[]{:S(2)}, u32[]{:S(2)}) collective-permute-start(bf16[8,1,128,1024]{2,3,0,1:T(8,128)(2,1)} %copy-done.1), channel_id=1, source_target_pairs={{0,8},{8,16},{16,24},{1,9},{9,17},{17,25},{2,10},{10,18},{18,26},{... | collective-permute-start | bytes 6291464 | tf_op jit(solution)/shard_map/ppermute | solution.py:17
  84.9 4.1 %copy.24 = f32[8,1,128,1024]{3,2,0,1:T(8,128)} copy(bf16[8,1,128,1024]{2,3,0,1:T(8,128)(2,1)} %copy.23) | data formatting | bytes 6291456 | tf_op jit(solution)/shard_map/convert_element_type | solution.py:50
  89.0 0.1 multiply_exponential_fusion
  89.1 0.1 fusion.28
  89.2 82.6 %all-to-all-done.1 = f32[8,8,128,128]{2,0,3,1:T(8,128)} async-done(((f32[8,8,128,128]{2,0,3,1:T(8,128)}), f32[8,8,128,128]{2,0,3,1:T(8,128)}, u32[]{:S(2)}, u32[]{:S(2)}) %all-to-all-start.1) | async-done | bytes 4194336 | tf_op jit(solution)/shard_map/all_to_all | solution.py:64
  171.8 3.1 %copy.30 = f32[8,8,128,128]{2,3,1,0:T(8,128)S(1)} copy(f32[8,8,128,128]{2,0,3,1:T(8,128)} %all-to-all-done.1) | data formatting | bytes 8388608 | tf_op jit(solution)/shard_map/all_to_all | solution.py:64
  174.9 0.0 collective-permute-done
  174.9 0.0 collective-permute-done.1
  174.9 0.0 copy-start.4
  175.0 15.0 %fusion.3 = bf16[8,1,128,1024]{2,3,0,1:T(8,128)(2,1)S(1)} fusion(f32[8,8,128,128]{2,3,1,0:T(8,128)S(1)} %copy.30, bf16[8,1,128,1024]{2,3,0,1:T(8,128)(2,1)} %collective-permute-done.1, bf16[8,1,128,1024]{2,3,0,1:T(8,128)(2,1)S(1)} %copy-done.2, bf16[8,1,128,1024]{2,3,0,1:T(8,128)(2,1)} %collective-permute-done, f32[1024]{0:T(1024)S(1)} %bitcast.58, ...), kind=kLoop, calls=%fused_computation.31 | loop fusion | flops 69206016 | bytes 12652544 | tf_op jit(solution)/shard_map/convert_element_type | solution.py:65
  190.0 0.4 fusion
  190.4 1.9 fusion.2
  192.3 3.9 %copy.31 = bf16[8,1,128,1024]{3,2,0,1:T(8,128)(2,1)} copy(bf16[8,1,128,1024]{2,3,0,1:T(8,128)(2,1)} %fusion.2) | data formatting | bytes 4194304 | tf_op jit(solution)/shard_map/convert_element_type | solution.py:69
  196.2 5.9 %fusion.29 = f32[1024,1024]{1,0:T(8,128)} fusion(bf16[1024,1024]{1,0:T(8,128)(2,1)} %bitcast.54, bf16[1024,1024]{1,0:T(8,128)(2,1)S(1)} %copy-done), kind=kOutput, calls=%fused_computation.72 | convolution fusion | flops 2147483648 | bytes 8388608 | tf_op jit(solution)/shard_map/dot_general | solution.py:71
  202.1 11.1 %fusion.4 = bf16[1024,1024]{1,0:T(8,128)(2,1)} fusion(f32[8,1,128,1024]{3,2,0,1:T(8,128)} %copy.24, bf16[1024,1024]{1,0:T(8,128)(2,1)} %param.13, f32[1024,1024]{1,0:T(8,128)} %fusion.29, bf16[1024,1024]{1,0:T(8,128)(2,1)} %bitcast.55, bf16[1024,1024]{1,0:T(8,128)(2,1)} %param.12), kind=kOutput, calls=%fused_computation.33 | convolution fusion | flops 4303355904 | bytes 16777216 | tf_op jit(solution)/shard_map/dot_general | solution.py:74
  (13 shorter events, 0.1 us)
Async XLA Ops:
  0.0 196.2 %copy-start = (bf16[1024,1024]{1,0:T(8,128)(2,1)S(1)}, bf16[1024,1024]{1,0:T(8,128)(2,1)}, u32[]{:S(2)}) copy-start(bf16[1024,1024]{1,0:T(8,128)(2,1)} %param.11) | copy-start | bytes 6291460
  8.1 1.3 copy-start.1
  12.1 55.6 %all-to-all-start = ((bf16[8,1,128,1024]{2,0,1,3:T(8,128)(2,1)}), bf16[8,1,128,1024]{2,0,1,3:T(8,128)(2,1)}, u32[]{:S(2)}, u32[]{:S(2)}) async-start(bf16[8,1,128,1024]{2,0,1,3:T(8,128)(2,1)} %copy.25), calls=%async_computation | async-start | bytes 4194304 | tf_op jit(solution)/shard_map/all_to_all | solution.py:59
  74.7 97.1 %all-to-all-start.1 = ((f32[8,8,128,128]{2,0,3,1:T(8,128)}), f32[8,8,128,128]{2,0,3,1:T(8,128)}, u32[]{:S(2)}, u32[]{:S(2)}) async-start(f32[8,8,128,128]{2,0,3,1:T(8,128)} %copy.29), calls=%async_computation.1 | async-start | bytes 8388608 | tf_op jit(solution)/shard_map/all_to_all | solution.py:64
  79.2 9.8 %copy-start.3 = (f32[1024]{0:T(1024)S(1)}, f32[1024]{0:T(1024)}, u32[]{:S(2)}) copy-start(f32[1024]{0:T(1024)} %param.9) | copy-start | bytes 12292
  79.2 95.7 %collective-permute-start = (bf16[8,1,128,1024]{2,3,0,1:T(8,128)(2,1)}, bf16[8,1,128,1024]{2,3,0,1:T(8,128)(2,1)}, u32[]{:S(2)}, u32[]{:S(2)}) collective-permute-start(bf16[8,1,128,1024]{2,3,0,1:T(8,128)(2,1)} %copy-done.1), channel_id=1, source_target_pairs={{8,0},{16,8},{24,16},{9,1},{17,9},{25,17},{10,2},{18,10},{26,18},{... | collective-permute-start | bytes 6291464 | tf_op jit(solution)/shard_map/ppermute | solution.py:20
  80.5 94.4 %collective-permute-start.1 = (bf16[8,1,128,1024]{2,3,0,1:T(8,128)(2,1)}, bf16[8,1,128,1024]{2,3,0,1:T(8,128)(2,1)}, u32[]{:S(2)}, u32[]{:S(2)}) collective-permute-start(bf16[8,1,128,1024]{2,3,0,1:T(8,128)(2,1)} %copy-done.1), channel_id=1, source_target_pairs={{0,8},{8,16},{16,24},{1,9},{9,17},{17,25},{2,10},{10,18},{18,26},{... | collective-permute-start | bytes 6291464 | tf_op jit(solution)/shard_map/ppermute | solution.py:17
  171.8 3.2 %copy-start.2 = (bf16[8,1,128,1024]{2,3,0,1:T(8,128)(2,1)S(1)}, bf16[8,1,128,1024]{2,3,0,1:T(8,128)(2,1)}, u32[]{:S(2)}) copy-start(bf16[8,1,128,1024]{2,3,0,1:T(8,128)(2,1)} %copy-done.1) | copy-start | bytes 6291460
  174.9 15.5 %copy-start.4 = (f32[1024]{0:T(1024)S(1)}, f32[1024]{0:T(1024)}, u32[]{:S(2)}) copy-start(f32[1024]{0:T(1024)} %param.8) | copy-start | bytes 12292
where the time goes:
time: 214 us; the launch traced here: 213 us
  waiting for transfers between devices  129 us (60%)
  local copies, waits for them, and re-layouts  23.6 us (11%)
  other arithmetic  21.5 us (10%)
  matrix products  21.2 us (10%)
  starting transfers between devices  17.5 us (8%)
    all_to_all x1, waiting for transfers between devices, body(): lax.all_to_all(spatial_mix, 'sa', split_axis=1, concat_axis=3, tiled=True)  82.6 us
    all_to_all x1, waiting for transfers between devices, body(): lax.all_to_all(normed, 'sa', split_axis=3, concat_axis=1, tiled=True)  46.7 us
    convert_element_type x1, other arithmetic, body(): summed = (temporal_mix + spatial_mix).astype(jnp.bfloat16)  15 us
    dot_general x1, matrix products, body(): jnp.dot(hidden, w_down, preferred_element_type=jnp.float32)  11.1 us
    all_to_all x1, starting transfers between devices, body(): lax.all_to_all(normed, 'sa', split_axis=3, concat_axis=1, tiled=True)  7.28 us
    dot_general x1, matrix products, body(): gate_act = jnp.dot(flat_rows, w_gate, preferred_element_type=jnp.float32)  5.89 us
    unnamed x11, local copies, waits for them, and re-layouts  5.4 us
    all_to_all x1, starting transfers between devices, body(): lax.all_to_all(spatial_mix, 'sa', split_axis=1, concat_axis=3, tiled=True)  4.56 us
  transfers between devices with their start and end apart: 4, of which 2 were waited for; matrix products, arithmetic and copies ran while one was open for 4% of the time, Pallas kernels for 0%

commit v1 on v0

v1 whole, which is shorter than its diff:
```python
import functools

import jax
import jax.numpy as jnp
from jax import lax
from jax.experimental import pallas as pl
from jax.experimental.pallas import tpu as pltpu
from jax.sharding import PartitionSpec as P

EPS = 1e-06
MESH = pl.DeviceIdType.MESH
ROWS = 16
LANES = 128
COLS = 256
F32 = jnp.float32
BF16 = jnp.bfloat16


def loop(start, stop, step_fn):
    def step(i, carry):
        step_fn(i)
        return carry

    lax.fori_loop(start, stop, step, 0)


def aligned(index, size):
    return pl.ds(pl.multiple_of(index * size, size), size)


def kernel(
    n, nt, chunks,
    video_hbm, gain_ref, rate_ref, taps_ref, gate_hbm, up_hbm, down_hbm,
    out_hbm,
    video, normed, prev, after, got, mixed, back, time_mix, normal, hidden, out,
    w_gate, w_up, w_down, decay,
    load_sem, weight_sem, store_sem,
    fwd_send, fwd_recv, back_send, back_recv, halo_send, halo_recv,
):
    frames, width, channels = video.shape
    group = frames * width // n
    part = group // chunks
    cols = width // chunks
    me = lax.axis_index("sa")
    t = lax.axis_index("ta")
    per_frame = width // group
    tiles = channels // LANES

    def chunk_cols(c):
        return pl.ds(c * cols, cols)

    def place(p, c):
        start = lax.rem(p, per_frame) * group + c * part
        return p // per_frame, pl.ds(pl.multiple_of(start, part), part)

    loads = []
    for c in range(chunks):
        load = pltpu.make_async_copy(
            video_hbm.at[:, chunk_cols(c)], video.at[:, chunk_cols(c)], load_sem.at[c]
        )
        load.start()
        loads.append(load)

    barrier = pltpu.get_barrier_semaphore()

    def greet(o):
        pl.semaphore_signal(
            barrier, inc=1, device_id={"sa": lax.rem(me + o, n)}, device_id_type=MESH
        )

    loop(1, n, greet)

    @pl.when(t > 0)
    def _():
        pl.semaphore_signal(barrier, inc=1, device_id={"ta": t - 1}, device_id_type=MESH)

    @pl.when(t < nt - 1)
    def _():
        pl.semaphore_signal(barrier, inc=1, device_id={"ta": t + 1}, device_id_type=MESH)

    weights = []
    for i, (src, dst) in enumerate(((gate_hbm, w_gate), (up_hbm, w_up), (down_hbm, w_down))):
        load = pltpu.make_async_copy(src, dst, weight_sem.at[i])
        load.start()
        weights.append(load)

    for d in range(frames + 1):
        decay[d : d + 1, :] = jnp.exp(rate_ref[...] * (-float(d)))

    def norm_chunk(c):
        row_tiles = cols // ROWS

        def one(i):
            f = i // row_tiles
            rows = pl.ds(pl.multiple_of(c * cols + lax.rem(i, row_tiles) * ROWS, ROWS), ROWS)
            x = video[f, rows, :].astype(F32)
            scale = lax.rsqrt(jnp.mean(x * x, -1, keepdims=True) + EPS)
            normed[f, rows, :] = (x * scale).astype(BF16)

        loop(0, frames * row_tiles, one)

    def fwd_copy(p, c, slot_at_target):
        f, rows = place(p, c)
        return pltpu.make_async_remote_copy(
            src_ref=normed.at[f, rows],
            dst_ref=got.at[slot_at_target, pl.ds(c * part, part)],
            send_sem=fwd_send.at[c, p],
            recv_sem=fwd_recv.at[c, slot_at_target],
            device_id={"sa": p},
            device_id_type=MESH,
        )

    def back_copy(p, c, owner):
        f, rows = place(owner, c)
        return pltpu.make_async_remote_copy(
            src_ref=mixed.at[p, pl.ds(c * part, part)],
            dst_ref=back.at[f, rows],
            send_sem=back_send.at[c, p],
            recv_sem=back_recv.at[c, owner],
            device_id={"sa": p},
            device_id_type=MESH,
        )

    def halo_copy(c, up):
        dst = prev if up else after
        return pltpu.make_async_remote_copy(
            src_ref=normed.at[:, chunk_cols(c)],
            dst_ref=dst.at[:, chunk_cols(c)],
            send_sem=halo_send.at[c, int(up)],
            recv_sem=halo_recv.at[c, int(up)],
            device_id={"ta": t + 1 if up else t - 1},
            device_id_type=MESH,
        )

    for c in range(chunks):
        loads[c].wait()
        norm_chunk(c)
        if c == 0:
            greeted = (t > 0).astype(jnp.int32) + (t < nt - 1).astype(jnp.int32)
            pl.semaphore_wait(barrier, n - 1 + greeted)
        loop(1, n, lambda o, c=c: fwd_copy(lax.rem(me + o, n), c, me).start())

        @pl.when(t > 0)
        def _(c=c):
            halo_copy(c, False).start()

        @pl.when(t < nt - 1)
        def _(c=c):
            halo_copy(c, True).start()

    @pl.when(t == 0)
    def _():
        prev[...] = jnp.zeros_like(prev)

    @pl.when(t == nt - 1)
    def _():
        after[...] = jnp.zeros_like(after)

    def mix_chunk(c):
        own_f, own_rows = place(me, c)
        got[me, pl.ds(c * part, part), :] = normed[own_f, own_rows, :]

        def one(i):
            lanes = aligned(lax.rem(i, tiles), LANES)
            rows = pl.ds(pl.multiple_of(c * part + i // tiles * ROWS, ROWS), ROWS)
            if n <= 8:
                taps = [taps_ref[j, :, lanes] for j in range(2 * n - 1)]
                x = [got[k, rows, lanes].astype(F32) for k in range(n)]
                for h in range(n):
                    total = taps[h + n - 1] * x[0]
                    for k in range(1, n):
                        total = total + taps[h - k + n - 1] * x[k]
                    mixed[h, rows, lanes] = total.astype(BF16)
            else:
                def one_row(h):
                    def add(k, total):
                        tap = taps_ref[h - k + n - 1, :, lanes]
                        return total + tap * got[k, rows, lanes].astype(F32)

                    total = lax.fori_loop(0, n, add, jnp.zeros((ROWS, LANES), F32))
                    mixed[h, rows, lanes] = total.astype(BF16)

                loop(0, n, one_row)

        loop(0, part // ROWS * tiles, one)
        back[own_f, own_rows, :] = mixed[me, pl.ds(c * part, part), :]

    def time_chunk(c):
        last = frames - 1

        def one(i):
            lanes = aligned(lax.rem(i, tiles), LANES)
            rows = pl.ds(pl.multiple_of(c * cols + i // tiles * ROWS, ROWS), ROWS)
            a = [decay[d : d + 1, lanes] for d in range(frames + 1)]
            x = [normed[f, rows, lanes].astype(F32) for f in range(frames)]
            total = list(x)
            inner = jnp.zeros((ROWS, LANES), F32)
            for f in range(1, frames):
                inner = a[1] * (inner + x[f - 1])
                total[f] = total[f] + inner
            inner = jnp.zeros((ROWS, LANES), F32)
            for f in range(last - 1, -1, -1):
                inner = a[1] * (inner + x[f + 1])
                total[f] = total[f] + inner
            outer = jnp.zeros((ROWS, LANES), F32)
            for f in range(last, -1, -1):
                outer = outer + a[frames - f] * prev[f, rows, lanes].astype(F32)
                total[f] = total[f] + a[f] * outer
            outer = jnp.zeros((ROWS, LANES), F32)
            for f in range(frames):
                outer = outer + a[f + 1] * after[f, rows, lanes].astype(F32)
                total[f] = total[f] + a[last - f] * outer
            for f in range(frames):
                time_mix[f, rows, lanes] = total[f]

        loop(0, cols // ROWS * tiles, one)

    for c in range(chunks):
        loop(1, n, lambda o, c=c: fwd_copy(me, c, lax.rem(me + n - o, n)).wait_recv())
        mix_chunk(c)
        loop(1, n, lambda o, c=c: back_copy(lax.rem(me + o, n), c, me).start())

        @pl.when(t > 0)
        def _(c=c):
            halo_copy(c, True).wait_recv()

        @pl.when(t < nt - 1)
        def _(c=c):
            halo_copy(c, False).wait_recv()

        time_chunk(c)

    for load in weights:
        load.wait()

    block = max(256 // cols, 1)
    height = block * cols

    def feed_chunk(c):
        row_tiles = cols // ROWS

        def one(i):
            f = i // row_tiles
            rows = pl.ds(pl.multiple_of(c * cols + lax.rem(i, row_tiles) * ROWS, ROWS), ROWS)
            summed = (time_mix[f, rows, :] + back[f, rows, :].astype(F32)).astype(BF16)
            x = summed.astype(F32)
            scale = lax.rsqrt(jnp.mean(x * x, -1, keepdims=True) + EPS)
            normal[aligned(i, ROWS), :] = (x * scale * gain_ref[...]).astype(BF16)

        loop(0, frames * row_tiles, one)

        def blocks(b):
            flat = aligned(b, height)

            def widen(j):
                at = aligned(j, COLS)
                x = normal[flat, :]
                gate = jnp.dot(x, w_gate[:, at], preferred_element_type=F32)
                up = jnp.dot(x, w_up[:, at], preferred_element_type=F32)
                hidden[:, at] = (jax.nn.silu(gate) * up).astype(BF16)

            loop(0, w_gate.shape[1] // COLS, widen)

            def narrow(j):
                at = aligned(j, COLS)
                y = jnp.dot(hidden[...], w_down[:, at], preferred_element_type=F32)
                here = (pl.ds(b * block, block), chunk_cols(c), at)
                total = video[here].astype(F32) + y.reshape(block, cols, COLS)
                out[here] = total.astype(BF16)

            loop(0, channels // COLS, narrow)

        loop(0, frames // block, blocks)

    stores = []
    for c in range(chunks):
        loop(1, n, lambda o, c=c: back_copy(me, c, lax.rem(me + n - o, n)).wait_recv())
        feed_chunk(c)
        store = pltpu.make_async_copy(
            out.at[:, chunk_cols(c)], out_hbm.at[:, chunk_cols(c)], store_sem.at[c]
        )
        store.start()
        stores.append(store)

    for c in range(chunks):
        def sent(o, c=c):
            p = lax.rem(me + o, n)
            fwd_copy(p, c, me).wait_send()
            back_copy(p, c, me).wait_send()

        loop(1, n, sent)

        @pl.when(t > 0)
        def _(c=c):
            halo_copy(c, False).wait_send()

        @pl.when(t < nt - 1)
        def _(c=c):
            halo_copy(c, True).wait_send()

        stores[c].wait()


def body(n, nt, video, mix_gain, t_rate, s_kernel, w_gate, w_up, w_down):
    frames, _, width, channels = video.shape
    hid = w_gate.shape[1]
    group = frames * width // n
    chunks = 4 if group == width else 1
    cols = width // chunks
    height = max(256 // cols, 1) * cols
    clip = (frames, width, channels)
    sem = pltpu.SemaphoreType.DMA
    vmem = pl.BlockSpec(memory_space=pltpu.VMEM)
    hbm = pl.BlockSpec(memory_space=pl.ANY)
    tokens = frames * width
    result = pl.pallas_call(
        functools.partial(kernel, n, nt, chunks),
        out_shape=jax.ShapeDtypeStruct(clip, BF16),
        in_specs=[hbm, vmem, vmem, vmem, hbm, hbm, hbm],
        out_specs=hbm,
        scratch_shapes=[
            pltpu.VMEM(clip, BF16),
            pltpu.VMEM(clip, BF16),
            pltpu.VMEM(clip, BF16),
            pltpu.VMEM(clip, BF16),
            pltpu.VMEM((n, group, channels), BF16),
            pltpu.VMEM((n, group, channels), BF16),
            pltpu.VMEM(clip, BF16),
            pltpu.VMEM(clip, F32),
            pltpu.VMEM((frames * cols, channels), BF16),
            pltpu.VMEM((height, hid), BF16),
            pltpu.VMEM(clip, BF16),
            pltpu.VMEM((channels, hid), BF16),
            pltpu.VMEM((channels, hid), BF16),
            pltpu.VMEM((hid, channels), BF16),
            pltpu.VMEM((frames + 8, channels), F32),
            sem((chunks,)),
            sem((3,)),
            sem((chunks,)),
            sem((chunks, n)),
            sem((chunks, n)),
            sem((chunks, n)),
            sem((chunks, n)),
            sem((chunks, 2)),
            sem((chunks, 2)),
        ],
        compiler_params=pltpu.CompilerParams(
            collective_id=0, has_side_effects=True, vmem_limit_bytes=52 * 2**20
        ),
        cost_estimate=pl.CostEstimate(
            flops=6 * tokens * channels * hid,
            bytes_accessed=4 * tokens * channels + 6 * channels * hid,
            transcendentals=tokens * hid,
        ),
    )(
        video.reshape(clip),
        mix_gain.reshape(1, channels),
        t_rate.reshape(1, channels),
        s_kernel.reshape(-1, 1, channels),
        w_gate,
        w_up,
        w_down,
    )
    return result.reshape(video.shape)


def solution(mesh):
    in_specs = (P("ta", "sa", None, None), P(), P(), P(), P(), P(), P())
    return jax.shard_map(
        functools.partial(body, mesh.shape["sa"], mesh.shape["ta"]),
        mesh=mesh,
        in_specs=in_specs,
        out_specs=P("ta", "sa", None, None),
        check_vma=False,
    )
```

time: 214 us -> 108 us (0.50)
  waiting for transfers between devices: 129 us -> 0 us
  Pallas kernels: 0 us -> 102 us
  other arithmetic: 21.5 us -> 0 us
  matrix products: 21.2 us -> 0 us
  local copies, waits for them, and re-layouts: 23.6 us -> 5.33 us
  starting transfers between devices: 17.5 us -> 0 us
    all_to_all x2 -> x0, waiting for transfers between devices: 129 us -> none  [the longest x1 82.6 us: body(): lax.all_to_all(spatial_mix, 'sa', split_axis=1, concat_axis=3, tiled=True)]
    pallas_call x0 -> x1, Pallas kernels: none -> 102 us  [body(): pl.pallas_call(functools.partial(kernel, n, nt, chunks), out_shape=jax.Sh...]
    dot_general x3 -> x0, matrix products: 21.2 us -> none  [the longest x1 11.1 us: body(): jnp.dot(hidden, w_down, preferred_element_type=jnp.float32)]
    convert_element_type x4 -> x0, other arithmetic: 18.9 us -> none  [the longest x1 15 us: body(): summed = (temporal_mix + spatial_mix).astype(jnp.bfloat16)]
    all_to_all x2 -> x0, starting transfers between devices: 11.8 us -> none  [the longest x1 7.28 us: body(): lax.all_to_all(normed, 'sa', split_axis=3, concat_axis=1, tiled=True)]
    convert_element_type x3 -> x0, local copies, waits for them, and re-layouts: 10.7 us -> none  [the longest x1 4.1 us: body(): widened_in = video.astype(jnp.float32)]
    ppermute x2 -> x0, starting transfers between devices: 5.65 us -> none  [the longest x1 4.36 us: padded_2(): lax.ppermute(lax.slice_in_dim(block, block.shape[dim] - width, None, axis...]
    all_to_all x1 -> x0, local copies, waits for them, and re-layouts: 3.15 us -> none  [body(): lax.all_to_all(spatial_mix, 'sa', split_axis=1, concat_axis=3, tiled=True)]
  transfers between devices with their start and end apart: 4 -> 0, of which waited for: 2 -> 0; matrix products, arithmetic and copies ran while one was open for 4% -> 0% of each run, Pallas kernels for 0% -> 0%
where the time goes in v1:
time: 108 us; the launch traced here: 107 us
  Pallas kernels  102 us (94%)
  local copies, waits for them, and re-layouts  5.33 us (5%)
    pallas_call x1, Pallas kernels, body(): pl.pallas_call(functools.partial(kernel, n, nt, chunks), out_shape=jax.Sh...  102 us
    unnamed x5, local copies, waits for them, and re-layouts  4.45 us

profile of v1, /device:TPU:0, one launch (start us, length us, event | category | flops | bytes accessed | tf_op | source)
XLA Modules:
  0.0 107.3 jit_solution(17262481167583189920)
XLA Ops:
  0.0 0.9 reshape.18.taps_ref
  0.9 0.0 copy-start
  0.9 0.7 copy-done
  1.6 0.0 copy-start.1
  1.6 0.7 copy-done.1
  2.3 101.9 %shard_map.73 = bf16[8,128,1024]{2,1,0:T(8,128)(2,1)} custom-call(bf16[8,128,1024]{2,1,0:T(8,128)(2,1)} %bitcast.9, f32[1,1024]{1,0:T(1,128)S(1)} %bitcast.6, f32[1,1024]{1,0:T(1,128)S(1)} %bitcast.7, f32[15,1,1024]{2,1,0:T(1,128)S(1)} %reshape.18.taps_ref, bf16[1024,1024]{1,0:T(8,128)(2,1)} %gate_hbm.1, bf16[1024,1024]{1,0:T(8,128)(2,1)} %up_hbm.1, ...), custom_call_target="tpu_custom_call" | custom-call | flops 6442450944 | bytes 10485760 | tf_op jit(solution)/shard_map/pallas_call | solution.py:316
  104.2 3.1 %copy.10 = bf16[8,1,128,1024]{3,2,1,0:T(8,128)(2,1)} copy(bf16[8,1,128,1024]{3,2,1,0:T(8,128)(2,1)} %bitcast.8) | data formatting | bytes 4194304
Async XLA Ops:
  0.9 0.7 copy-start
  1.6 0.7 copy-start.1

commit v2 on v1

--- a/solution.py
+++ b/solution.py
@@ -29,30 +29,48 @@
 
 
 def kernel(
-    n, nt, chunks,
-    video_hbm, gain_ref, rate_ref, taps_ref, gate_hbm, up_hbm, down_hbm,
-    out_hbm,
-    video, normed, prev, after, got, mixed, back, time_mix, normal, hidden, out,
-    w_gate, w_up, w_down, decay,
-    load_sem, weight_sem, store_sem,
+    n, nt, pieces,
+    video_hbm, gain_hbm, rate_hbm, taps_hbm, gate_hbm, up_hbm, down_hbm,
+    out,
+    video, normed, prev, after, got, mixed, back, time_mix, normal, hidden,
+    gain_ref, rate_ref, taps_ref, w_gate, w_up, w_down, decay,
+    load_sem, small_sem, weight_sem,
     fwd_send, fwd_recv, back_send, back_recv, halo_send, halo_recv,
 ):
     frames, width, channels = video.shape
     group = frames * width // n
-    part = group // chunks
-    cols = width // chunks
+    chunks = len(pieces)
     me = lax.axis_index("sa")
     t = lax.axis_index("ta")
     per_frame = width // group
     tiles = channels // LANES
 
     def chunk_cols(c):
-        return pl.ds(c * cols, cols)
+        return pl.ds(*pieces[c])
+
+    def chunk_part(c):
+        return pl.ds(pieces[c][0] * group // width, pieces[c][1] * group // width)
+
+    def peer(o):
+        p, bit = me, 1
+        while bit < n:
+            p = p + lax.rem(o // bit, 2) * (1 - 2 * lax.rem(me // bit, 2)) * bit
+            bit *= 2
+        return p
+
+    def each_peer(step_fn):
+        loop(1, n, lambda i: step_fn(peer(n - i)))
 
     def place(p, c):
-        start = lax.rem(p, per_frame) * group + c * part
-        return p // per_frame, pl.ds(pl.multiple_of(start, part), part)
-
+        rows = chunk_part(c)
+        start = lax.rem(p, per_frame) * group + rows.start
+        return p // per_frame, pl.ds(pl.multiple_of(start, ROWS), rows.size)
+
+    smalls = []
+    for i, (src, dst) in enumerate(
+        ((rate_hbm, rate_ref), (taps_hbm, taps_ref), (gain_hbm, gain_ref))
+    ):
+        smalls.append(pltpu.make_async_copy(src, dst, small_sem.at[i]))
     loads = []
     for c in range(chunks):
         load = pltpu.make_async_copy(
@@ -61,14 +79,15 @@
         load.start()
         loads.append(load)
 
+    for load in smalls:
+        load.start()
+
     barrier = pltpu.get_barrier_semaphore()
 
-    def greet(o):
-        pl.semaphore_signal(
-            barrier, inc=1, device_id={"sa": lax.rem(me + o, n)}, device_id_type=MESH
-        )
-
-    loop(1, n, greet)
+    def greet(p):
+        pl.semaphore_signal(barrier, inc=1, device_id={"sa": p}, device_id_type=MESH)
+
+    each_peer(greet)
 
     @pl.when(t > 0)
     def _():
@@ -84,15 +103,13 @@
         load.start()
         weights.append(load)
 
-    for d in range(frames + 1):
-        decay[d : d + 1, :] = jnp.exp(rate_ref[...] * (-float(d)))
-
     def norm_chunk(c):
+        first, cols = pieces[c]
         row_tiles = cols // ROWS
 
         def one(i):
             f = i // row_tiles
-            rows = pl.ds(pl.multiple_of(c * cols + lax.rem(i, row_tiles) * ROWS, ROWS), ROWS)
+            rows = pl.ds(pl.multiple_of(first + lax.rem(i, row_tiles) * ROWS, ROWS), ROWS)
             x = video[f, rows, :].astype(F32)
             scale = lax.rsqrt(jnp.mean(x * x, -1, keepdims=True) + EPS)
             normed[f, rows, :] = (x * scale).astype(BF16)
@@ -103,7 +120,7 @@
         f, rows = place(p, c)
         return pltpu.make_async_remote_copy(
             src_ref=normed.at[f, rows],
-            dst_ref=got.at[slot_at_target, pl.ds(c * part, part)],
+            dst_ref=got.at[slot_at_target, chunk_part(c)],
             send_sem=fwd_send.at[c, p],
             recv_sem=fwd_recv.at[c, slot_at_target],
             device_id={"sa": p},
@@ -113,7 +130,7 @@
     def back_copy(p, c, owner):
         f, rows = place(owner, c)
         return pltpu.make_async_remote_copy(
-            src_ref=mixed.at[p, pl.ds(c * part, part)],
+            src_ref=mixed.at[p, chunk_part(c)],
             dst_ref=back.at[f, rows],
             send_sem=back_send.at[c, p],
             recv_sem=back_recv.at[c, owner],
@@ -138,7 +155,7 @@
         if c == 0:
             greeted = (t > 0).astype(jnp.int32) + (t < nt - 1).astype(jnp.int32)
             pl.semaphore_wait(barrier, n - 1 + greeted)
-        loop(1, n, lambda o, c=c: fwd_copy(lax.rem(me + o, n), c, me).start())
+        each_peer(lambda p, c=c: fwd_copy(p, c, me).start())
 
         @pl.when(t > 0)
         def _(c=c):
@@ -147,6 +164,12 @@
         @pl.when(t < nt - 1)
         def _(c=c):
             halo_copy(c, True).start()
+
+    for load in smalls:
+        load.wait()
+
+    for d in range(frames + 1):
+        decay[d : d + 1, :] = jnp.exp(rate_ref[...] * (-float(d)))
 
     @pl.when(t == 0)
     def _():
@@ -158,13 +181,14 @@
 
     def mix_chunk(c):
         own_f, own_rows = place(me, c)
-        got[me, pl.ds(c * part, part), :] = normed[own_f, own_rows, :]
+        part = chunk_part(c)
+        got[me, part, :] = normed[own_f, own_rows, :]
 
         def one(i):
             lanes = aligned(lax.rem(i, tiles), LANES)
-            rows = pl.ds(pl.multiple_of(c * part + i // tiles * ROWS, ROWS), ROWS)
+            rows = pl.ds(pl.multiple_of(part.start + i // tiles * ROWS, ROWS), ROWS)
             if n <= 8:
-                taps = [taps_ref[j, :, lanes] for j in range(2 * n - 1)]
+                taps = [taps_ref[j : j + 1, lanes] for j in range(2 * n - 1)]
                 x = [got[k, rows, lanes].astype(F32) for k in range(n)]
                 for h in range(n):
                     total = taps[h + n - 1] * x[0]
@@ -182,15 +206,16 @@
 
                 loop(0, n, one_row)
 
-        loop(0, part // ROWS * tiles, one)
-        back[own_f, own_rows, :] = mixed[me, pl.ds(c * part, part), :]
+        loop(0, part.size // ROWS * tiles, one)
+        back[own_f, own_rows, :] = mixed[me, part, :]
 
     def time_chunk(c):
         last = frames - 1
+        first, cols = pieces[c]
 
         def one(i):
             lanes = aligned(lax.rem(i, tiles), LANES)
-            rows = pl.ds(pl.multiple_of(c * cols + i // tiles * ROWS, ROWS), ROWS)
+            rows = pl.ds(pl.multiple_of(first + i // tiles * ROWS, ROWS), ROWS)
             a = [decay[d : d + 1, lanes] for d in range(frames + 1)]
             x = [normed[f, rows, lanes].astype(F32) for f in range(frames)]
             total = list(x)
@@ -216,9 +241,9 @@
         loop(0, cols // ROWS * tiles, one)
 
     for c in range(chunks):
-        loop(1, n, lambda o, c=c: fwd_copy(me, c, lax.rem(me + n - o, n)).wait_recv())
+        each_peer(lambda p, c=c: fwd_copy(p, c, p).wait_recv())
         mix_chunk(c)
-        loop(1, n, lambda o, c=c: back_copy(lax.rem(me + o, n), c, me).start())
+        each_peer(lambda p, c=c: back_copy(p, c, me).start())
 
         @pl.when(t > 0)
         def _(c=c):
@@ -233,21 +258,22 @@
     for load in weights:
         load.wait()
 
-    block = max(256 // cols, 1)
-    height = block * cols
-
     def feed_chunk(c):
+        first, cols = pieces[c]
         row_tiles = cols // ROWS
 
         def one(i):
             f = i // row_tiles
-            rows = pl.ds(pl.multiple_of(c * cols + lax.rem(i, row_tiles) * ROWS, ROWS), ROWS)
+            rows = pl.ds(pl.multiple_of(first + lax.rem(i, row_tiles) * ROWS, ROWS), ROWS)
             summed = (time_mix[f, rows, :] + back[f, rows, :].astype(F32)).astype(BF16)
             x = summed.astype(F32)
             scale = lax.rsqrt(jnp.mean(x * x, -1, keepdims=True) + EPS)
             normal[aligned(i, ROWS), :] = (x * scale * gain_ref[...]).astype(BF16)
 
         loop(0, frames * row_tiles, one)
+
+        block = min(max(256 // cols, 1), frames)
+        height = block * cols
 
         def blocks(b):
             flat = aligned(b, height)
@@ -257,13 +283,13 @@
                 x = normal[flat, :]
                 gate = jnp.dot(x, w_gate[:, at], preferred_element_type=F32)
                 up = jnp.dot(x, w_up[:, at], preferred_element_type=F32)
-                hidden[:, at] = (jax.nn.silu(gate) * up).astype(BF16)
+                hidden[:height, at] = (jax.nn.silu(gate) * up).astype(BF16)
 
             loop(0, w_gate.shape[1] // COLS, widen)
 
             def narrow(j):
                 at = aligned(j, COLS)
-                y = jnp.dot(hidden[...], w_down[:, at], preferred_element_type=F32)
+                y = jnp.dot(hidden[:height, :], w_down[:, at], preferred_element_type=F32)
                 here = (pl.ds(b * block, block), chunk_cols(c), at)
                 total = video[here].astype(F32) + y.reshape(block, cols, COLS)
                 out[here] = total.astype(BF16)
@@ -272,23 +298,16 @@
 
         loop(0, frames // block, blocks)
 
-    stores = []
-    for c in range(chunks):
-        loop(1, n, lambda o, c=c: back_copy(me, c, lax.rem(me + n - o, n)).wait_recv())
+    for c in range(chunks):
+        each_peer(lambda p, c=c: back_copy(p, c, p).wait_recv())
         feed_chunk(c)
-        store = pltpu.make_async_copy(
-            out.at[:, chunk_cols(c)], out_hbm.at[:, chunk_cols(c)], store_sem.at[c]
-        )
-        store.start()
-        stores.append(store)
-
-    for c in range(chunks):
-        def sent(o, c=c):
-            p = lax.rem(me + o, n)
+
+    for c in range(chunks):
+        def sent(p, c=c):
             fwd_copy(p, c, me).wait_send()
             back_copy(p, c, me).wait_send()
 
-        loop(1, n, sent)
+        each_peer(sent)
 
         @pl.when(t > 0)
         def _(c=c):
@@ -297,27 +316,28 @@
         @pl.when(t < nt - 1)
         def _(c=c):
             halo_copy(c, True).wait_send()
-
-        stores[c].wait()
 
 
 def body(n, nt, video, mix_gain, t_rate, s_kernel, w_gate, w_up, w_down):
     frames, _, width, channels = video.shape
     hid = w_gate.shape[1]
     group = frames * width // n
-    chunks = 4 if group == width else 1
-    cols = width // chunks
-    height = max(256 // cols, 1) * cols
+    eighths = [1, 2, 2, 2, 1] if group == width else [8]
+    sizes = [width * e // 8 for e in eighths]
+    chunks = len(sizes)
+    pieces = [(sum(sizes[:c]), sizes[c]) for c in range(chunks)]
+    most = max(sizes)
+    height = min(max(256 // most, 1), frames) * most
+    taps = s_kernel if n <= 8 else s_kernel.reshape(-1, 1, channels)
     clip = (frames, width, channels)
     sem = pltpu.SemaphoreType.DMA
-    vmem = pl.BlockSpec(memory_space=pltpu.VMEM)
-    hbm = pl.BlockSpec(memory_space=pl.ANY)
+    hbm = pl.BlockSpec(memory_space=pltpu.HBM)
     tokens = frames * width
     result = pl.pallas_call(
-        functools.partial(kernel, n, nt, chunks),
+        functools.partial(kernel, n, nt, pieces),
         out_shape=jax.ShapeDtypeStruct(clip, BF16),
-        in_specs=[hbm, vmem, vmem, vmem, hbm, hbm, hbm],
-        out_specs=hbm,
+        in_specs=[hbm] * 7,
+        out_specs=pl.BlockSpec(memory_space=pltpu.VMEM),
         scratch_shapes=[
             pltpu.VMEM(clip, BF16),
             pltpu.VMEM(clip, BF16),
@@ -327,16 +347,18 @@
             pltpu.VMEM((n, group, channels), BF16),
             pltpu.VMEM(clip, BF16),
             pltpu.VMEM(clip, F32),
-            pltpu.VMEM((frames * cols, channels), BF16),
+            pltpu.VMEM((frames * most, channels), BF16),
             pltpu.VMEM((height, hid), BF16),
-            pltpu.VMEM(clip, BF16),
+            pltpu.VMEM((1, channels), F32),
+            pltpu.VMEM((1, channels), F32),
+            pltpu.VMEM(taps.shape, F32),
             pltpu.VMEM((channels, hid), BF16),
             pltpu.VMEM((channels, hid), BF16),
             pltpu.VMEM((hid, channels), BF16),
             pltpu.VMEM((frames + 8, channels), F32),
             sem((chunks,)),
             sem((3,)),
-            sem((chunks,)),
+            sem((3,)),
             sem((chunks, n)),
             sem((chunks, n)),
             sem((chunks, n)),
@@ -345,7 +367,7 @@
             sem((chunks, 2)),
         ],
         compiler_params=pltpu.CompilerParams(
-            collective_id=0, has_side_effects=True, vmem_limit_bytes=52 * 2**20
+            collective_id=0, has_side_effects=True, vmem_limit_bytes=60 * 2**20
         ),
         cost_estimate=pl.CostEstimate(
             flops=6 * tokens * channels * hid,
@@ -356,7 +378,7 @@
         video.reshape(clip),
         mix_gain.reshape(1, channels),
         t_rate.reshape(1, channels),
-        s_kernel.reshape(-1, 1, channels),
+        taps,
         w_gate,
         w_up,
         w_down,

time: 108 us -> 110 us (1.019)
  Pallas kernels: 102 us -> 107 us
  local copies, waits for them, and re-layouts: 5.33 us -> 3.08 us
    pallas_call x1, Pallas kernels: 102 us -> 107 us  [body(): pl.pallas_call(functools.partial(kernel, n, nt, pieces), out_shape=jax.Sh...]
    unnamed x5 -> x1, local copies, waits for them, and re-layouts: 4.45 us -> 3.08 us
where the time goes in v2:
time: 110 us
  Pallas kernels  107 us (97%)
  local copies, waits for them, and re-layouts  3.08 us (3%)
    pallas_call x1, Pallas kernels, body(): pl.pallas_call(functools.partial(kernel, n, nt, pieces), out_shape=jax.Sh...  107 us
    unnamed x1, local copies, waits for them, and re-layouts  3.08 us

profile of v2, /device:TPU:0, one launch (start us, length us, event | category | flops | bytes accessed | tf_op | source)
XLA Modules:
  0.0 110.2 jit_solution(5646948242806571654)
XLA Ops:
  0.0 107.1 %shard_map.73 = bf16[8,128,1024]{2,1,0:T(8,128)(2,1)} custom-call(bf16[8,128,1024]{2,1,0:T(8,128)(2,1)} %bitcast.7, f32[1,1024]{1,0:T(1,128)} %bitcast.8, f32[1,1024]{1,0:T(1,128)} %bitcast.9, f32[15,1024]{1,0:T(8,128)} %taps_hbm.1, bf16[1024,1024]{1,0:T(8,128)(2,1)} %gate_hbm.1, bf16[1024,1024]{1,0:T(8,128)(2,1)} %up_hbm.1, bf16[1024,1024]{1,0:T(8,128)(2,1)} %down_hbm.1), custom_call_target="tpu_custom_call" | custom-call | flops 6442450944 | bytes 10485760 | tf_op jit(solution)/shard_map/pallas_call | solution.py:336
  107.1 3.1 %copy.10 = bf16[8,1,128,1024]{3,2,1,0:T(8,128)(2,1)} copy(bf16[8,1,128,1024]{3,2,1,0:T(8,128)(2,1)} %bitcast.6) | data formatting | bytes 4194304

commit v3 on v2

--- a/solution.py
+++ b/solution.py
@@ -52,10 +52,7 @@
         return pl.ds(pieces[c][0] * group // width, pieces[c][1] * group // width)
 
     def peer(o):
-        p, bit = me, 1
-        while bit < n:
-            p = p + lax.rem(o // bit, 2) * (1 - 2 * lax.rem(me // bit, 2)) * bit
-            bit *= 2
+        p = lax.rem(me + n - o, n)
         return p
 
     def each_peer(step_fn):
@@ -322,7 +319,7 @@
     frames, _, width, channels = video.shape
     hid = w_gate.shape[1]
     group = frames * width // n
-    eighths = [1, 2, 2, 2, 1] if group == width else [8]
+    eighths = [2, 2, 2, 2] if group == width else [8]
     sizes = [width * e // 8 for e in eighths]
     chunks = len(sizes)
     pieces = [(sum(sizes[:c]), sizes[c]) for c in range(chunks)]

time: 110 us -> 106 us (0.964)
  Pallas kernels: 107 us -> 103 us
    pallas_call x1, Pallas kernels: 107 us -> 103 us  [body(): pl.pallas_call(functools.partial(kernel, n, nt, pieces), out_shape=jax.Sh...]
where the time goes in v3:
time: 106 us
  Pallas kernels  103 us (97%)
  local copies, waits for them, and re-layouts  3.08 us (3%)
    pallas_call x1, Pallas kernels, body(): pl.pallas_call(functools.partial(kernel, n, nt, pieces), out_shape=jax.Sh...  103 us
    unnamed x1, local copies, waits for them, and re-layouts  3.08 us

profile of v3, /device:TPU:0, one launch (start us, length us, event | category | flops | bytes accessed | tf_op | source)
XLA Modules:
  0.0 105.9 jit_solution(8039149369610780914)
XLA Ops:
  0.0 102.8 %shard_map.73 = bf16[8,128,1024]{2,1,0:T(8,128)(2,1)} custom-call(bf16[8,128,1024]{2,1,0:T(8,128)(2,1)} %bitcast.7, f32[1,1024]{1,0:T(1,128)} %bitcast.8, f32[1,1024]{1,0:T(1,128)} %bitcast.9, f32[15,1024]{1,0:T(8,128)} %taps_hbm.1, bf16[1024,1024]{1,0:T(8,128)(2,1)} %gate_hbm.1, bf16[1024,1024]{1,0:T(8,128)(2,1)} %up_hbm.1, bf16[1024,1024]{1,0:T(8,128)(2,1)} %down_hbm.1), custom_call_target="tpu_custom_call" | custom-call | flops 6442450944 | bytes 10485760 | tf_op jit(solution)/shard_map/pallas_call | solution.py:333
  102.8 3.1 %copy.10 = bf16[8,1,128,1024]{3,2,1,0:T(8,128)(2,1)} copy(bf16[8,1,128,1024]{3,2,1,0:T(8,128)(2,1)} %bitcast.6) | data formatting | bytes 4194304
